TPU v7x, 32 devices: a whole 2x2x4 slice. The times are simulated.
32 devices in a mesh: parts: 2 (over x), attn: 8 (over z, y), ffn: 2 (over core).
Axes of the slice: x: 2, y: 2, z: 4, core: 2. Of those that a mesh axis runs over, the one named last changes fastest.
Arguments:
- hidden_states: bfloat16 [256, 7168], P(('parts', 'attn', 'ffn')), parts along dimension 0, may hold values from -127 to 127
- norm_gain: bfloat16 [7168], replicated, may hold values from 0.099609375 to 1.8984375
- expert_ids: int32 [256, 3], P(('parts', 'attn', 'ffn')), parts along dimension 0, may hold values from 0 to 3, as said below
- route_weight: float32 [256, 3], P(('parts', 'attn', 'ffn')), parts along dimension 0, may hold values from 0.2 to 1
- w_gate: bfloat16 [7168, 16384], P(None, ('attn', 'ffn')), may hold values from -0.0625 to 0.0625
- w_up: bfloat16 [7168, 16384], P(None, ('attn', 'ffn')), may hold values from -0.0625 to 0.0625
- w_down: bfloat16 [16384, 7168], P(('attn', 'ffn')), may hold values from -0.09375 to 0.09375
- queries: bfloat16 [256, 16384], P(('parts', 'attn', 'ffn')), parts along dimension 0, may hold values from -36 to 36
- key_cache: bfloat16 [256, 128, 256], P(('parts', 'attn', 'ffn')), parts along dimension 0, may hold values from -19 to 19
- value_cache: bfloat16 [256, 128, 256], P(('parts', 'attn', 'ffn')), parts along dimension 0, may hold values from -6 to 6
- lengths: int32 [256], P(('parts', 'attn', 'ffn')), parts along dimension 0, may hold values from 2 to 128, as said below
Outputs:
- ffn_out: bfloat16 [256, 7168], P(('parts', 'attn', 'ffn')), parts along dimension 0
- attn_out: bfloat16 [256, 16384], P(('parts', 'attn', 'ffn')), parts along dimension 0
There are 2 independent parts, one for each index of `parts`. A program takes and returns all parts, laid end to end along the dimension named above; an argument that names none is the same for every part. Nothing has to cross between parts.
Inputs may be any that keep to these rules, and one draw needn't show every extreme that they name: `expert_ids`: each row names 3 different experts. Among the 8 rows of one device at most 7 name any one expert, and in every draw one expert is named by exactly 7 rows on every device. `lengths`: each device has one row with exactly 128 filled slots.
All inputs are finite; a program needn't handle non-finite values.
Results may differ from a plain program's by a relative error of at most 0.0071.
Values may be sent and summed in bfloat16 or wider, within the bound.
A program may use at most 128 MiB of HBM per device.

v0:
```python
import jax
import jax.numpy as jnp
from jax import lax
from jax.sharding import PartitionSpec as P

EXPERTS = 4
HEADS = 64
HEAD_DIM = 256
CAP = 7


def on_device(
    hidden_states,
    norm_gain,
    expert_ids,
    route_weight,
    w_gate,
    w_up,
    w_down,
    queries,
    key_cache,
    value_cache,
    lengths,
):
    row_count, features = hidden_states.shape
    devices = lax.axis_size(("attn", "ffn"))
    group_size = devices // EXPERTS
    as_float = hidden_states.astype(jnp.float32)
    mean_square = jnp.mean(as_float * as_float, axis=-1, keepdims=True)
    normed = (as_float * lax.rsqrt(mean_square + 1e-06) * norm_gain.astype(jnp.float32)).astype(
        jnp.bfloat16
    )
    matches = expert_ids[:, :, None] == jnp.arange(EXPERTS, dtype=jnp.int32)[None, None, :]
    row_weight = jnp.sum(jnp.where(matches, route_weight[:, :, None], 0.0), axis=1)
    is_named = jnp.any(matches, axis=1).T
    slot_count = CAP
    counted = is_named.astype(jnp.int32)
    earlier = jnp.cumsum(counted, axis=1) - counted
    selection = is_named[:, None, :] & (
        earlier[:, None, :] == jnp.arange(slot_count, dtype=jnp.int32)[None, :, None]
    )
    packed = jnp.einsum(
        "ecr,rd->ecd", selection.astype(jnp.bfloat16), normed, preferred_element_type=jnp.float32
    ).astype(jnp.bfloat16)
    slot_weight = jnp.sum(jnp.where(selection, row_weight.T[:, None, :], 0.0), axis=2)

    def expert_partial(arrived):
        flat_rows = arrived.reshape(-1, features)
        gate_part = jnp.dot(flat_rows, w_gate, preferred_element_type=jnp.float32)
        up_part = jnp.dot(flat_rows, w_up, preferred_element_type=jnp.float32)
        expert_hidden = (jax.nn.silu(gate_part) * up_part).astype(jnp.bfloat16)
        partial_rows = jnp.dot(expert_hidden, w_down, preferred_element_type=jnp.float32).astype(
            jnp.bfloat16
        )
        return partial_rows.reshape(arrived.shape)

    def bring_home(partial_rows):
        slot_total = partial_rows.shape[1]
        returned = lax.all_to_all(
            partial_rows, ("attn", "ffn"), split_axis=0, concat_axis=0, tiled=True
        )
        return jnp.sum(
            returned.reshape(EXPERTS, group_size, slot_total, features).astype(jnp.float32), axis=1
        )

    outgoing = jnp.repeat(packed, group_size, axis=0)
    expert_sums = (lambda arrived: bring_home(expert_partial(arrived)))(
        lax.all_to_all(outgoing, ("attn", "ffn"), split_axis=0, concat_axis=0, tiled=True)
    )
    weighted = expert_sums * slot_weight[:, :, None]
    ffn_out = jnp.einsum(
        "ecr,ecd->rd", selection.astype(jnp.float32), weighted, precision=lax.Precision.HIGHEST
    ).astype(jnp.bfloat16)
    query_heads = queries.reshape(row_count, HEADS, HEAD_DIM)
    scores = jnp.einsum(
        "rhd,rld->rhl", query_heads, key_cache, preferred_element_type=jnp.float32
    ) * HEAD_DIM ** (-0.5)
    visible = (
        jnp.arange(key_cache.shape[1], dtype=jnp.int32)[None, None, :] < lengths[:, None, None]
    )
    top_score = jnp.max(jnp.where(visible, scores, -1e30), axis=-1, keepdims=True)
    raised = jnp.where(visible, jnp.exp(scores - top_score), 0.0)
    attention_probs = (raised / jnp.sum(raised, axis=-1, keepdims=True)).astype(jnp.bfloat16)
    mixed = jnp.einsum(
        "rhl,rld->rhd", attention_probs, value_cache, preferred_element_type=jnp.float32
    )
    attn_out = mixed.reshape(row_count, HEADS * HEAD_DIM).astype(jnp.bfloat16)
    return (ffn_out, attn_out)


def solution(mesh):
    in_specs = (
        P(("parts", "attn", "ffn"), None),
        P(),
        P(("parts", "attn", "ffn"), None),
        P(("parts", "attn", "ffn"), None),
        P(None, ("attn", "ffn")),
        P(None, ("attn", "ffn")),
        P(("attn", "ffn"), None),
        P(("parts", "attn", "ffn"), None),
        P(("parts", "attn", "ffn"), None, None),
        P(("parts", "attn", "ffn"), None, None),
        P(("parts", "attn", "ffn")),
    )
    out_specs = (P(("parts", "attn", "ffn"), None), P(("parts", "attn", "ffn"), None))
    return jax.shard_map(
        on_device, mesh=mesh, in_specs=in_specs, out_specs=out_specs, check_vma=False
    )
```

profile of v0, /device:TPU:15, one launch (start us, length us, event | category | flops | bytes accessed | tf_op | source)
XLA Modules:
  0.0 128.9 jit_solution(1727209001427077767)
XLA Ops:
  0.6 0.0 copy-start
  0.6 0.8 fusion.34
  1.4 0.2 reduce_window_sum.11
  1.6 0.7 convert_element_type.43
  2.3 1.1 fusion.16
  3.4 1.3 %convolution_convert_fusion.1 = bf16[4,7,7168]{2,1,0:T(8,128)(2,1)S(1)} fusion(bf16[8,7168]{1,0:T(8,128)(2,1)} %param.11, f32[7168]{0:T(1024)S(1)} %convert_element_type.43, f32[8]{0:T(128)S(1)} %add_rsqrt_fusion, s32[4,8]{1,0:T(4,128)S(1)} %convert_subtract_fusion, pred[4,8]{1,0:T(4,128)(4,1)S(1)} %bitcast.29), kind=kOutput, calls=%fused_computation.2 | convolution fusion | flops 3641792 | bytes 544960 | tf_op jit(solution)/shard_map/ecr,rd->ecd/dot_general | solution.py:42
  4.7 0.2 broadcast_in_dim.59
  4.9 48.1 %all_to_all.10 = bf16[16,7,7168]{2,1,0:T(8,128)(2,1)} all-to-all(bf16[16,7,7168]{2,1,0:T(8,128)(2,1)S(1)} %bitcast.26), channel_id=1, replica_groups=mesh['parts'=2,'attn'=8,'ffn'=2] {'attn','ffn'}, dimensions={0} | all-to-all | bytes 3211264 | tf_op jit(solution)/shard_map/all_to_all | solution.py:68
  53.0 1.8 %reshape.60 = bf16[112,7168]{1,0:T(8,128)(2,1)S(1)} reshape(bf16[16,7,7168]{2,1,0:T(8,128)(2,1)} %all_to_all.10) | data formatting | bytes 3211264 | tf_op jit(solution)/shard_map/reshape | solution.py:48
  54.9 7.3 %fusion.38 = f32[112,1024]{1,0:T(8,128)S(1)} fusion(bf16[112,7168]{1,0:T(8,128)(2,1)S(1)} %reshape.60, bf16[7168,1024]{1,0:T(8,128)(2,1)} %param.15), kind=kOutput, calls=%fused_computation.54 | convolution fusion | flops 1644167168 | bytes 16744448 | tf_op jit(solution)/shard_map/dot_general | solution.py:49
  62.2 14.9 %convolution_convert_fusion = bf16[112,7168]{1,0:T(8,128)(2,1)} fusion(bf16[1024,7168]{1,0:T(8,128)(2,1)} %param.17, bf16[112,7168]{1,0:T(8,128)(2,1)S(1)} %reshape.60, bf16[7168,1024]{1,0:T(8,128)(2,1)} %param.16, f32[112,1024]{1,0:T(8,128)S(1)} %fusion.38), kind=kOutput, calls=%fused_computation.1 | convolution fusion | flops 3289825280 | bytes 33030144 | tf_op jit(solution)/shard_map/dot_general | solution.py:52
  77.0 0.0 copy-start.5
  77.0 0.0 copy-start.1
  77.0 0.0 copy-start.2
  77.0 2.8 %reshape.61 = bf16[16,7,7168]{2,1,0:T(8,128)(2,1)} reshape(bf16[112,7168]{1,0:T(8,128)(2,1)} %convolution_convert_fusion) | data formatting | bytes 3211264 | tf_op jit(solution)/shard_map/reshape | solution.py:55
  79.8 0.0 copy-start.3
  79.8 5.3 %all-to-all-start.1 = ((bf16[16,7,7168]{2,1,0:T(8,128)(2,1)}), bf16[16,7,7168]{2,1,0:T(8,128)(2,1)S(1)}, u32[]{:S(2)}, u32[]{:S(2)}) async-start(bf16[16,7,7168]{2,1,0:T(8,128)(2,1)} %reshape.61), calls=%async_computation.1 | async-start | bytes 3670016 | tf_op jit(solution)/shard_map/all_to_all | solution.py:59
  85.1 0.0 copy-done.5
  85.1 0.1 iota_compare_fusion.2
  85.2 0.0 copy-done.1
  85.2 0.0 copy-done.2
  85.2 0.3 convolution_multiply_fusion.1
  85.5 1.4 %fusion.37 = (f32[8,64]{1,0:T(8,128)S(1)}, f32[8,64,128]{2,1,0:T(8,128)S(1)}) fusion(f32[8,64,128]{2,1,0:T(8,128)S(1)} %convolution_multiply_fusion.1, pred[8,128]{1,0:T(8,128)(4,1)S(1)} %iota_compare_fusion.2), kind=kOutput, calls=%fused_computation.53 | output fusion | flops 262271 | bytes 527360 | tf_op jit(solution)/shard_map/sub | solution.py:82
  86.9 0.0 copy-done
  86.9 0.3 fusion.3
  87.2 0.9 copy.24
  88.1 0.0 copy-done.3
  88.1 0.0 copy-done.4
  88.1 0.1 select_reduce_fusion.1
  88.2 38.7 %all-to-all-done.1 = bf16[16,7,7168]{2,1,0:T(8,128)(2,1)S(1)} async-done(((bf16[16,7,7168]{2,1,0:T(8,128)(2,1)}), bf16[16,7,7168]{2,1,0:T(8,128)(2,1)S(1)}, u32[]{:S(2)}, u32[]{:S(2)}) %all-to-all-start.1) | async-done | bytes 1605664 | tf_op jit(solution)/shard_map/all_to_all | solution.py:59
  126.9 0.4 convert_reduce_fusion
  127.3 1.7 %fusion.1 = bf16[8,7168]{1,0:T(8,128)(2,1)} fusion(f32[4,7,7168]{2,1,0:T(8,128)S(1)} %convert_reduce_fusion, f32[4,7]{1,0:T(4,128)S(1)} %select_reduce_fusion.1, s32[4,8]{1,0:T(4,128)S(1)} %convert_subtract_fusion, pred[4,8]{1,0:T(4,128)(4,1)S(1)} %bitcast.31), kind=kOutput, calls=%fused_computation.4 | convolution fusion | flops 19526080 | bytes 917776 | tf_op jit(solution)/shard_map/ecr,ecd->rd/dot_general | solution.py:71
  (5 shorter events, 0.0 us)
Async XLA Ops:
  0.6 86.3 %copy-start = (bf16[8,128,256]{2,1,0:T(8,128)(2,1)S(1)}, bf16[8,128,256]{2,1,0:T(8,128)(2,1)}, u32[]{:S(2)}) copy-start(bf16[8,128,256]{2,1,0:T(8,128)(2,1)} %param.20) | copy-start | bytes 1572868
  77.0 8.1 %copy-start.5 = (s32[8]{0:T(128)S(1)}, s32[8]{0:T(128)}, u32[]{:S(2)}) copy-start(s32[8]{0:T(128)} %param.21) | copy-start | bytes 100
  77.0 8.2 %copy-start.1 = (bf16[8,128,256]{2,1,0:T(8,128)(2,1)S(1)}, bf16[8,128,256]{2,1,0:T(8,128)(2,1)}, u32[]{:S(2)}) copy-start(bf16[8,128,256]{2,1,0:T(8,128)(2,1)} %param.19) | copy-start | bytes 1572868
  77.0 8.2 %copy-start.2 = (bf16[8,16384]{1,0:T(8,128)(2,1)S(1)}, bf16[8,16384]{1,0:T(8,128)(2,1)}, u32[]{:S(2)}) copy-start(bf16[8,16384]{1,0:T(8,128)(2,1)} %param.18) | copy-start | bytes 786436
  79.8 8.2 %copy-start.3 = (s32[8,3]{0,1:T(4,128)S(1)}, s32[8,3]{0,1:T(4,128)}, u32[]{:S(2)}) copy-start(s32[8,3]{0,1:T(4,128)} %param.13) | copy-start | bytes 292
  79.8 8.2 %copy-start.4 = (f32[8,3]{0,1:T(4,128)S(1)}, f32[8,3]{0,1:T(4,128)}, u32[]{:S(2)}) copy-start(f32[8,3]{0,1:T(4,128)} %param.14) | copy-start | bytes 292
  79.8 47.1 %all-to-all-start.1 = ((bf16[16,7,7168]{2,1,0:T(8,128)(2,1)}), bf16[16,7,7168]{2,1,0:T(8,128)(2,1)S(1)}, u32[]{:S(2)}, u32[]{:S(2)}) async-start(bf16[16,7,7168]{2,1,0:T(8,128)(2,1)} %reshape.61), calls=%async_computation.1 | async-start | bytes 3670016 | tf_op jit(solution)/shard_map/all_to_all | solution.py:59
where the time goes:
time: 129 us
  blocking collectives  48.1 us (37%)
  waiting for transfers between devices  38.7 us (30%)
  matrix products  25.7 us (20%)
  local copies, waits for them, and re-layouts  5.68 us (4%)
  starting transfers between devices  5.26 us (4%)
  other arithmetic  4.73 us (4%)
    all_to_all x1, blocking collectives, on_device(): lax.all_to_all(outgoing, ('attn', 'ffn'), split_axis=0, concat_axis=0, ti...  48.1 us
    all_to_all x1, waiting for transfers between devices, bring_home(): lax.all_to_all(partial_rows, ('attn', 'ffn'), split_axis=0, concat_axis=0...  38.7 us
    dot_general x1, matrix products, expert_partial(): jnp.dot(expert_hidden, w_down, preferred_element_type=jnp.float32)  14.9 us
    dot_general x1, matrix products, expert_partial(): gate_part = jnp.dot(flat_rows, w_gate, preferred_element_type=jnp.float32)  7.28 us
    all_to_all x1, starting transfers between devices, bring_home(): lax.all_to_all(partial_rows, ('attn', 'ffn'), split_axis=0, concat_axis=0...  5.26 us
    reshape x1, local copies, waits for them, and re-layouts, expert_partial(): return partial_rows.reshape(arrived.shape)  2.8 us
  transfers between devices with their start and end apart: 1, of which 1 were waited for; matrix products, arithmetic and copies ran while one was open for 2% of the time, Pallas kernels for 0%

commit v1 on v0

v1 whole, which is shorter than its diff:
```python
import functools

import jax
import jax.numpy as jnp
from jax import lax
from jax.experimental import pallas as pl
from jax.experimental.pallas import tpu as pltpu
from jax.sharding import PartitionSpec as P

EXPERTS = 4
HEADS = 64
HEAD_DIM = 256
ROWS = 8
PIECES = 4
CHUNKS = 7
F32 = jnp.float32
BF16 = jnp.bfloat16
MESH = pl.DeviceIdType.MESH


def kernel(
    outer,
    hid_ref,
    gain_ref,
    ids_ref,
    rw_ref,
    len_ref,
    q_hbm,
    k_hbm,
    v_hbm,
    wg_hbm,
    wu_hbm,
    wd_hbm,
    ffn_ref,
    attn_ref,
    wg,
    wu,
    wd,
    q_v,
    k_v,
    v_v,
    x,
    gate_acc,
    up_acc,
    hidden,
    part,
    core_in,
    sum_core,
    y_in,
    sum_y,
    z_in,
    att_sem,
    wgu_sem,
    wd_sem,
    z_send,
    z_recv,
    y_send,
    y_recv,
    c_send,
    c_recv,
    rc_send,
    rc_recv,
    ry_send,
    ry_recv,
    rz_send,
    rz_recv,
):
    parts = lax.axis_index("parts")
    attn = lax.axis_index("attn")
    c = lax.axis_index("ffn")
    o = attn // 2
    i = attn % 2
    half = hid_ref.shape[1] // 2
    kc = half // CHUNKS
    blocks = 4 * outer

    def device(o2, i2, c2):
        return (parts, o2 * 2 + i2, c2)

    def z_peer(d):
        return lax.rem(o + d, outer)

    def att_copies():
        return [
            pltpu.make_async_copy(a, b, att_sem.at[n])
            for n, (a, b) in enumerate(((q_hbm, q_v), (k_hbm, k_v), (v_hbm, v_v)))
        ]

    def in_weights(k):
        copies = []
        for h in range(2):
            rows = pl.ds(pl.multiple_of(h * half + k * kc, kc), kc)
            for n, (a, b) in enumerate(((wg_hbm, wg), (wu_hbm, wu))):
                copies.append(
                    pltpu.make_async_copy(
                        a.at[rows, :], b.at[k, pl.ds(h * kc, kc), :], wgu_sem.at[k, n, h]
                    )
                )
        return copies

    def out_weights(k):
        copies = []
        for h in range(2):
            cols = pl.ds(pl.multiple_of(h * half + k * kc, kc), kc)
            copies.append(
                pltpu.make_async_copy(
                    wd_hbm.at[:, cols], wd.at[k, :, pl.ds(h * kc, kc)], wd_sem.at[k, h]
                )
            )
        return copies

    def z_copy(k, o_slot, d):
        return pltpu.make_async_remote_copy(
            src_ref=x.at[k, c, i, o_slot],
            dst_ref=x.at[k, c, i, o_slot],
            send_sem=z_send.at[k, d],
            recv_sem=z_recv.at[k, o_slot],
            device_id=device(z_peer(d), i, c),
            device_id_type=MESH,
        )

    def y_copy(k, i_slot):
        return pltpu.make_async_remote_copy(
            src_ref=x.at[k, c, i_slot],
            dst_ref=x.at[k, c, i_slot],
            send_sem=y_send.at[k],
            recv_sem=y_recv.at[k],
            device_id=device(o, 1 - i, c),
            device_id_type=MESH,
        )

    def c_copy(k, c_slot):
        return pltpu.make_async_remote_copy(
            src_ref=x.at[k, c_slot],
            dst_ref=x.at[k, c_slot],
            send_sem=c_send.at[k],
            recv_sem=c_recv.at[k],
            device_id=device(o, i, 1 - c),
            device_id_type=MESH,
        )

    def rc_copy(k):
        return pltpu.make_async_remote_copy(
            src_ref=part.at[k, 1 - c],
            dst_ref=core_in.at[k],
            send_sem=rc_send.at[k],
            recv_sem=rc_recv.at[k],
            device_id=device(o, i, 1 - c),
            device_id_type=MESH,
        )

    def ry_copy(k):
        return pltpu.make_async_remote_copy(
            src_ref=sum_core.at[k, 1 - i],
            dst_ref=y_in.at[k],
            send_sem=ry_send.at[k],
            recv_sem=ry_recv.at[k],
            device_id=device(o, 1 - i, c),
            device_id_type=MESH,
        )

    def rz_copy(k, o_src, o_dst, o_slot, d):
        return pltpu.make_async_remote_copy(
            src_ref=sum_y.at[k, o_src],
            dst_ref=z_in.at[k, o_slot],
            send_sem=rz_send.at[k, d],
            recv_sem=rz_recv.at[k, o_slot],
            device_id=device(o_dst, i, c),
            device_id_type=MESH,
        )

    for k in range(2):
        for copy in in_weights(k):
            copy.start()

    barrier = pltpu.get_barrier_semaphore()
    for d in range(1, outer):
        pl.semaphore_signal(
            barrier, inc=1, device_id=device(z_peer(d), i, c), device_id_type=MESH
        )
    pl.semaphore_signal(barrier, inc=1, device_id=device(o, 1 - i, c), device_id_type=MESH)
    pl.semaphore_signal(barrier, inc=1, device_id=device(o, i, 1 - c), device_id_type=MESH)

    for copy in att_copies():
        copy.start()

    as_float = hid_ref[...].astype(F32)
    mean_square = jnp.mean(as_float * as_float, axis=-1, keepdims=True)
    normed = as_float * lax.rsqrt(mean_square + 1e-06) * gain_ref[...]
    for k in range(CHUNKS):
        low = normed[:, k * kc : (k + 1) * kc]
        high = normed[:, half + k * kc : half + (k + 1) * kc]
        x[k, c, i, o] = jnp.concatenate([low, high], axis=0).astype(BF16)

    pl.semaphore_wait(barrier, outer + 1)

    def start_z(k, _):
        for d in range(1, outer):
            z_copy(k, o, d).start()
        return 0

    lax.fori_loop(0, CHUNKS, start_z, 0)

    def start_in(k, _):
        for copy in in_weights(k):
            copy.start()
        return 0

    lax.fori_loop(2, CHUNKS, start_in, 0)

    def start_out(k, _):
        for copy in out_weights(k):
            copy.start()
        return 0

    lax.fori_loop(0, CHUNKS, start_out, 0)

    gate_acc[...] = jnp.zeros_like(gate_acc)
    up_acc[...] = jnp.zeros_like(up_acc)
    for copy in att_copies():
        copy.wait()

    heads = HEADS // PIECES
    tall = heads * ROWS
    slots = k_v.shape[1]

    def attention(p):
        def columns(j):
            return pl.ds(pl.multiple_of((p * heads + j) * HEAD_DIM, HEAD_DIM), HEAD_DIM)

        query = jnp.concatenate(
            [q_v[:, columns(j)].astype(F32) for j in range(heads)], axis=0
        ).astype(BF16)
        row = lax.broadcasted_iota(jnp.int32, (tall, slots), 0) & (ROWS - 1)
        filled = jnp.zeros((tall, slots), jnp.int32)
        scores = jnp.zeros((tall, slots), F32)
        for r in range(ROWS):
            own = lax.dot_general(
                query, k_v[r], (((1,), (1,)), ((), ())), preferred_element_type=F32
            )
            scores = jnp.where(row == r, own, scores)
            filled = jnp.where(row == r, len_ref[r], filled)
        scores = scores * HEAD_DIM ** (-0.5)
        visible = lax.broadcasted_iota(jnp.int32, (tall, slots), 1) < filled
        top = jnp.max(jnp.where(visible, scores, -1e30), axis=-1, keepdims=True)
        raised = jnp.where(visible, jnp.exp(scores - top), 0.0)
        probs = raised / jnp.sum(raised, axis=-1, keepdims=True)
        mixed = jnp.zeros((tall, HEAD_DIM), F32)
        for r in range(ROWS):
            own = jnp.where(row == r, probs, 0.0).astype(BF16)
            mixed = mixed + jnp.dot(own, v_v[r], preferred_element_type=F32)
        for j in range(heads):
            attn_ref[:, columns(j)] = mixed[j * ROWS : (j + 1) * ROWS].astype(BF16)

    def gather_step(t, _):
        @pl.when(t < PIECES)
        def _():
            attention(t)

        @pl.when(t < CHUNKS)
        def _():
            for d in range(1, outer):
                z_copy(t, z_peer(d), d).wait_recv()
            y_copy(t, i).start()

        @pl.when((t >= 1) & (t < CHUNKS + 1))
        def _():
            y_copy(t - 1, 1 - i).wait_recv()
            c_copy(t - 1, c).start()

        @pl.when(t >= 2)
        def _():
            k = t - 2
            c_copy(k, 1 - c).wait_recv()
            for copy in in_weights(k):
                copy.wait()
            block = x[k].astype(F32).reshape(blocks, 2 * ROWS, kc)
            low = block[:, :ROWS, :].reshape(blocks * ROWS, kc).astype(BF16)
            high = block[:, ROWS:, :].reshape(blocks * ROWS, kc).astype(BF16)
            rows = jnp.concatenate([low, high], axis=1)
            gate_acc[...] += jnp.dot(rows, wg[k], preferred_element_type=F32)
            up_acc[...] += jnp.dot(rows, wu[k], preferred_element_type=F32)

        return 0

    lax.fori_loop(0, CHUNKS + 2, gather_step, 0)

    gate = gate_acc[...]
    hidden[...] = (gate / (1.0 + jnp.exp(-gate)) * up_acc[...]).astype(BF16)

    ids = ids_ref[...]
    weights = rw_ref[...]
    row_weight = [
        jnp.sum(jnp.where(ids == e, weights, 0.0), axis=1, keepdims=True) for e in range(EXPERTS)
    ]
    row_weight = [jnp.concatenate([w, w], axis=0) for w in row_weight]
    per_expert = outer // EXPERTS

    def sum_step(t, _):
        @pl.when(t < CHUNKS)
        def _():
            for copy in out_weights(t):
                copy.wait()
            down = jnp.dot(hidden[...], wd[t], preferred_element_type=F32)
            low = down[:, :kc].reshape(blocks, ROWS, kc)
            high = down[:, kc:].reshape(blocks, ROWS, kc)
            both = jnp.concatenate([low, high], axis=1).astype(BF16)
            part[t] = both.reshape(2, 2 * outer, 2 * ROWS, kc)
            rc_copy(t).start()

        @pl.when((t >= 1) & (t < CHUNKS + 1))
        def _():
            k = t - 1
            rc_copy(k).wait_recv()
            total = part[k, c].astype(F32) + core_in[k].astype(F32)
            sum_core[k] = total.astype(BF16).reshape(2, outer, 2 * ROWS, kc)
            ry_copy(k).start()

        @pl.when((t >= 2) & (t < CHUNKS + 2))
        def _():
            k = t - 2
            ry_copy(k).wait_recv()
            total = sum_core[k, i].astype(F32) + y_in[k].astype(F32)
            sum_y[k] = total.astype(BF16)
            z_in[k, o] = sum_y[k, o]
            for d in range(1, outer):
                rz_copy(k, z_peer(d), z_peer(d), o, d).start()

        @pl.when(t >= 3)
        def _():
            k = t - 3
            for d in range(1, outer):
                rz_copy(k, z_peer(d), z_peer(d), z_peer(d), d).wait_recv()
            total = jnp.zeros((2 * ROWS, kc), F32)
            for e in range(EXPERTS):
                expert = z_in[k, e * per_expert].astype(F32)
                for m in range(1, per_expert):
                    expert = expert + z_in[k, e * per_expert + m].astype(F32)
                total = total + row_weight[e] * expert
            ffn_ref[:, pl.ds(pl.multiple_of(k * kc, kc), kc)] = total[:ROWS].astype(BF16)
            ffn_ref[:, pl.ds(pl.multiple_of(half + k * kc, kc), kc)] = total[ROWS:].astype(BF16)

        return 0

    lax.fori_loop(0, CHUNKS + 3, sum_step, 0)

    def drain(k, _):
        for d in range(1, outer):
            z_copy(k, o, d).wait_send()
            rz_copy(k, z_peer(d), z_peer(d), o, d).wait_send()
        y_copy(k, i).wait_send()
        c_copy(k, c).wait_send()
        rc_copy(k).wait_send()
        ry_copy(k).wait_send()
        return 0

    lax.fori_loop(0, CHUNKS, drain, 0)


def on_device(
    hidden_states,
    norm_gain,
    expert_ids,
    route_weight,
    w_gate,
    w_up,
    w_down,
    queries,
    key_cache,
    value_cache,
    lengths,
):
    features = hidden_states.shape[1]
    units = w_gate.shape[1]
    outer = lax.axis_size("attn") // 2
    kc = features // 2 // CHUNKS
    blocks = 4 * outer
    vmem = pl.BlockSpec(memory_space=pltpu.VMEM)
    smem = pl.BlockSpec(memory_space=pltpu.SMEM)
    anywhere = pl.BlockSpec(memory_space=pl.ANY)
    dma = pltpu.SemaphoreType.DMA
    return pl.pallas_call(
        functools.partial(kernel, outer),
        out_shape=(
            jax.ShapeDtypeStruct(hidden_states.shape, BF16),
            jax.ShapeDtypeStruct(queries.shape, BF16),
        ),
        in_specs=[vmem] * 4 + [smem] + [anywhere] * 6,
        out_specs=(vmem, vmem),
        scratch_shapes=[
            pltpu.VMEM((CHUNKS, 2 * kc, units), BF16),
            pltpu.VMEM((CHUNKS, 2 * kc, units), BF16),
            pltpu.VMEM((CHUNKS, units, 2 * kc), BF16),
            pltpu.VMEM(queries.shape, BF16),
            pltpu.VMEM(key_cache.shape, BF16),
            pltpu.VMEM(value_cache.shape, BF16),
            pltpu.VMEM((CHUNKS, 2, 2, outer, 2 * ROWS, kc), BF16),
            pltpu.VMEM((blocks * ROWS, units), F32),
            pltpu.VMEM((blocks * ROWS, units), F32),
            pltpu.VMEM((blocks * ROWS, units), BF16),
            pltpu.VMEM((CHUNKS, 2, 2 * outer, 2 * ROWS, kc), BF16),
            pltpu.VMEM((CHUNKS, 2 * outer, 2 * ROWS, kc), BF16),
            pltpu.VMEM((CHUNKS, 2, outer, 2 * ROWS, kc), BF16),
            pltpu.VMEM((CHUNKS, outer, 2 * ROWS, kc), BF16),
            pltpu.VMEM((CHUNKS, outer, 2 * ROWS, kc), BF16),
            pltpu.VMEM((CHUNKS, outer, 2 * ROWS, kc), BF16),
            dma((3,)),
            dma((CHUNKS, 2, 2)),
            dma((CHUNKS, 2)),
            dma((CHUNKS, outer)),
            dma((CHUNKS, outer)),
            dma((CHUNKS,)),
            dma((CHUNKS,)),
            dma((CHUNKS,)),
            dma((CHUNKS,)),
            dma((CHUNKS,)),
            dma((CHUNKS,)),
            dma((CHUNKS,)),
            dma((CHUNKS,)),
            dma((CHUNKS, outer)),
            dma((CHUNKS, outer)),
        ],
        compiler_params=pltpu.CompilerParams(
            collective_id=0, has_side_effects=True, vmem_limit_bytes=60 * 2**20
        ),
    )(
        hidden_states,
        norm_gain.astype(F32).reshape(1, features),
        expert_ids,
        route_weight,
        lengths,
        queries,
        key_cache,
        value_cache,
        w_gate,
        w_up,
        w_down,
    )


def solution(mesh):
    in_specs = (
        P(("parts", "attn", "ffn"), None),
        P(),
        P(("parts", "attn", "ffn"), None),
        P(("parts", "attn", "ffn"), None),
        P(None, ("attn", "ffn")),
        P(None, ("attn", "ffn")),
        P(("attn", "ffn"), None),
        P(("parts", "attn", "ffn"), None),
        P(("parts", "attn", "ffn"), None, None),
        P(("parts", "attn", "ffn"), None, None),
        P(("parts", "attn", "ffn")),
    )
    out_specs = (P(("parts", "attn", "ffn"), None), P(("parts", "attn", "ffn"), None))
    return jax.shard_map(
        on_device, mesh=mesh, in_specs=in_specs, out_specs=out_specs, check_vma=False
    )
```

time: 129 us -> 64.2 us (0.50)
  the two profiles are of different devices: /device:TPU:15 before, /device:TPU:0 now
where the time goes in v1:
time: 64.2 us; the launch traced here: 63.9 us
  Pallas kernels  56 us (87%)
  local copies, waits for them, and re-layouts  5.91 us (9%)
  other arithmetic  1.32 us (2%)
    pallas_call x1, Pallas kernels, on_device(): pl.pallas_call(functools.partial(kernel, outer), out_shape=(jax.ShapeDtyp...  56 us
    unnamed x4, local copies, waits for them, and re-layouts  5.91 us
    reshape x1, other arithmetic, on_device(): norm_gain.astype(F32).reshape(1, features)  1.32 us

profile of v1, /device:TPU:0, one launch (start us, length us, event | category | flops | bytes accessed | tf_op | source)
XLA Modules:
  0.0 63.9 jit_solution(12189270220350421855)
XLA Ops:
  0.6 1.3 %copy.13.ids_ref = s32[8,3]{1,0:T(8,128)} copy(s32[8,3]{0,1:T(4,128)} %param.13) | data formatting | bytes 192 | tf_op args[2]
  2.0 1.3 %copy.14.rw_ref = f32[8,3]{1,0:T(8,128)} copy(f32[8,3]{0,1:T(4,128)} %param.14) | data formatting | bytes 192 | tf_op args[3]
  3.3 1.3 %reshape.11 = f32[7168]{0:T(1024)} convert(bf16[7168]{0:T(1024)(128)(2,1)} %param.12) | non-fusion elementwise | flops 7168 | bytes 43008 | tf_op jit(solution)/shard_map/reshape | solution.py:428
  4.6 56.0 %shard_map.122 = (bf16[8,7168]{1,0:T(8,128)(2,1)}, bf16[8,16384]{1,0:T(8,128)(2,1)}) custom-call(bf16[8,7168]{1,0:T(8,128)(2,1)} %hid_ref.1, f32[1,7168]{1,0:T(1,128)} %bitcast.1, s32[8,3]{1,0:T(8,128)} %copy.13.ids_ref, f32[8,3]{1,0:T(8,128)} %copy.14.rw_ref, s32[8]{0:T(128)} %len_ref.1, bf16[8,16384]{1,0:T(8,128)(2,1)} %q_hbm.1, ...), custom_call_target="tpu_custom_call" | custom-call | tf_op jit(solution)/shard_map/pallas_call | solution.py:382
  60.7 1.6 %copy.17 = bf16[8,7168]{1,0:T(8,128)(2,1)} copy(bf16[8,7168]{1,0:T(8,128)(2,1)} %get-tuple-element.4) | data formatting | bytes 229376
  62.2 1.7 %copy.18 = bf16[8,16384]{1,0:T(8,128)(2,1)} copy(bf16[8,16384]{1,0:T(8,128)(2,1)} %get-tuple-element.5) | data formatting | bytes 524288

commit v2 on v1

--- a/solution.py
+++ b/solution.py
@@ -13,6 +13,12 @@
 ROWS = 8
 PIECES = 4
 CHUNKS = 7
+AHEAD = 3
+GATHER_Y = 2
+GATHER_C = 4
+SUM_C = 1
+SUM_Y = 4
+SUM_Z = 7
 F32 = jnp.float32
 BF16 = jnp.bfloat16
 MESH = pl.DeviceIdType.MESH
@@ -119,12 +125,12 @@
             device_id_type=MESH,
         )
 
-    def y_copy(k, i_slot):
-        return pltpu.make_async_remote_copy(
-            src_ref=x.at[k, c, i_slot],
-            dst_ref=x.at[k, c, i_slot],
-            send_sem=y_send.at[k],
-            recv_sem=y_recv.at[k],
+    def y_copy(k, i_slot, o_slot):
+        return pltpu.make_async_remote_copy(
+            src_ref=x.at[k, c, i_slot, o_slot],
+            dst_ref=x.at[k, c, i_slot, o_slot],
+            send_sem=y_send.at[k, o_slot],
+            recv_sem=y_recv.at[k, o_slot],
             device_id=device(o, 1 - i, c),
             device_id_type=MESH,
         )
@@ -186,7 +192,7 @@
 
     as_float = hid_ref[...].astype(F32)
     mean_square = jnp.mean(as_float * as_float, axis=-1, keepdims=True)
-    normed = as_float * lax.rsqrt(mean_square + 1e-06) * gain_ref[...]
+    normed = as_float * lax.rsqrt(mean_square + 1e-06) * gain_ref[...].astype(F32).reshape(1, 2 * half)
     for k in range(CHUNKS):
         low = normed[:, k * kc : (k + 1) * kc]
         high = normed[:, half + k * kc : half + (k + 1) * kc]
@@ -197,9 +203,10 @@
     def start_z(k, _):
         for d in range(1, outer):
             z_copy(k, o, d).start()
-        return 0
-
-    lax.fori_loop(0, CHUNKS, start_z, 0)
+        y_copy(k, i, o).start()
+        return 0
+
+    lax.fori_loop(0, min(AHEAD, CHUNKS), start_z, 0)
 
     def start_in(k, _):
         for copy in in_weights(k):
@@ -261,16 +268,22 @@
         def _():
             for d in range(1, outer):
                 z_copy(t, z_peer(d), d).wait_recv()
-            y_copy(t, i).start()
-
-        @pl.when((t >= 1) & (t < CHUNKS + 1))
-        def _():
-            y_copy(t - 1, 1 - i).wait_recv()
-            c_copy(t - 1, c).start()
-
-        @pl.when(t >= 2)
-        def _():
-            k = t - 2
+                y_copy(t, i, z_peer(d)).start()
+
+        @pl.when(t + AHEAD < CHUNKS)
+        def _():
+            start_z(t + AHEAD, 0)
+
+        @pl.when((t >= GATHER_Y) & (t < CHUNKS + GATHER_Y))
+        def _():
+            k = t - GATHER_Y
+            for d in range(outer):
+                y_copy(k, 1 - i, z_peer(d)).wait_recv()
+            c_copy(k, c).start()
+
+        @pl.when(t >= GATHER_C)
+        def _():
+            k = t - GATHER_C
             c_copy(k, 1 - c).wait_recv()
             for copy in in_weights(k):
                 copy.wait()
@@ -283,17 +296,19 @@
 
         return 0
 
-    lax.fori_loop(0, CHUNKS + 2, gather_step, 0)
+    lax.fori_loop(0, CHUNKS + GATHER_C, gather_step, 0)
 
     gate = gate_acc[...]
     hidden[...] = (gate / (1.0 + jnp.exp(-gate)) * up_acc[...]).astype(BF16)
 
     ids = ids_ref[...]
     weights = rw_ref[...]
-    row_weight = [
-        jnp.sum(jnp.where(ids == e, weights, 0.0), axis=1, keepdims=True) for e in range(EXPERTS)
-    ]
-    row_weight = [jnp.concatenate([w, w], axis=0) for w in row_weight]
+    place = lax.broadcasted_iota(jnp.int32, (2 * ROWS, ROWS), 0) & (ROWS - 1)
+    diagonal = place == lax.broadcasted_iota(jnp.int32, (2 * ROWS, ROWS), 1)
+    row_weight = []
+    for e in range(EXPERTS):
+        along = jnp.sum(jnp.where(ids == e, weights, 0.0), axis=0, keepdims=True)
+        row_weight.append(jnp.sum(jnp.where(diagonal, along, 0.0), axis=1, keepdims=True))
     per_expert = outer // EXPERTS
 
     def sum_step(t, _):
@@ -308,17 +323,17 @@
             part[t] = both.reshape(2, 2 * outer, 2 * ROWS, kc)
             rc_copy(t).start()
 
-        @pl.when((t >= 1) & (t < CHUNKS + 1))
-        def _():
-            k = t - 1
+        @pl.when((t >= SUM_C) & (t < CHUNKS + SUM_C))
+        def _():
+            k = t - SUM_C
             rc_copy(k).wait_recv()
             total = part[k, c].astype(F32) + core_in[k].astype(F32)
             sum_core[k] = total.astype(BF16).reshape(2, outer, 2 * ROWS, kc)
             ry_copy(k).start()
 
-        @pl.when((t >= 2) & (t < CHUNKS + 2))
-        def _():
-            k = t - 2
+        @pl.when((t >= SUM_Y) & (t < CHUNKS + SUM_Y))
+        def _():
+            k = t - SUM_Y
             ry_copy(k).wait_recv()
             total = sum_core[k, i].astype(F32) + y_in[k].astype(F32)
             sum_y[k] = total.astype(BF16)
@@ -326,9 +341,9 @@
             for d in range(1, outer):
                 rz_copy(k, z_peer(d), z_peer(d), o, d).start()
 
-        @pl.when(t >= 3)
-        def _():
-            k = t - 3
+        @pl.when(t >= SUM_Z)
+        def _():
+            k = t - SUM_Z
             for d in range(1, outer):
                 rz_copy(k, z_peer(d), z_peer(d), z_peer(d), d).wait_recv()
             total = jnp.zeros((2 * ROWS, kc), F32)
@@ -342,13 +357,14 @@
 
         return 0
 
-    lax.fori_loop(0, CHUNKS + 3, sum_step, 0)
+    lax.fori_loop(0, CHUNKS + SUM_Z, sum_step, 0)
 
     def drain(k, _):
         for d in range(1, outer):
             z_copy(k, o, d).wait_send()
             rz_copy(k, z_peer(d), z_peer(d), o, d).wait_send()
-        y_copy(k, i).wait_send()
+        for d in range(outer):
+            y_copy(k, i, z_peer(d)).wait_send()
         c_copy(k, c).wait_send()
         rc_copy(k).wait_send()
         ry_copy(k).wait_send()
@@ -409,8 +425,8 @@
             dma((CHUNKS, 2)),
             dma((CHUNKS, outer)),
             dma((CHUNKS, outer)),
-            dma((CHUNKS,)),
-            dma((CHUNKS,)),
+            dma((CHUNKS, outer)),
+            dma((CHUNKS, outer)),
             dma((CHUNKS,)),
             dma((CHUNKS,)),
             dma((CHUNKS,)),
@@ -425,9 +441,9 @@
         ),
     )(
         hidden_states,
-        norm_gain.astype(F32).reshape(1, features),
-        expert_ids,
-        route_weight,
+        norm_gain,
+        expert_ids.T,
+        route_weight.T,
         lengths,
         queries,
         key_cache,

time: 64.2 us -> 48.8 us (0.76)
  Pallas kernels: 56 us -> 44.7 us
  local copies, waits for them, and re-layouts: 5.91 us -> 3.22 us
  other arithmetic: 1.32 us -> 0 us
    pallas_call x1, Pallas kernels: 56 us -> 44.7 us  [on_device(): pl.pallas_call(functools.partial(kernel, outer), out_shape=(jax.ShapeDtyp...]
    unnamed x4 -> x2, local copies, waits for them, and re-layouts: 5.91 us -> 3.22 us
    reshape x1 -> x0, other arithmetic: 1.32 us -> none  [on_device(): norm_gain.astype(F32).reshape(1, features)]
where the time goes in v2:
time: 48.8 us; the launch traced here: 48.6 us
  Pallas kernels  44.7 us (92%)
  local copies, waits for them, and re-layouts  3.22 us (7%)
  between operations  0.64 us (1%)
    pallas_call x1, Pallas kernels, on_device(): pl.pallas_call(functools.partial(kernel, outer), out_shape=(jax.ShapeDtyp...  44.7 us
    unnamed x2, local copies, waits for them, and re-layouts  3.22 us

profile of v2, /device:TPU:0, one launch (start us, length us, event | category | flops | bytes accessed | tf_op | source)
XLA Modules:
  0.0 48.6 jit_solution(18342899822456137038)
XLA Ops:
  0.6 44.7 %shard_map.122 = (bf16[8,7168]{1,0:T(8,128)(2,1)}, bf16[8,16384]{1,0:T(8,128)(2,1)}) custom-call(bf16[8,7168]{1,0:T(8,128)(2,1)} %hid_ref.1, bf16[7168]{0:T(1024)(128)(2,1)} %gain_ref.1, s32[3,8]{1,0:T(4,128)} %bitcast.2, f32[3,8]{1,0:T(4,128)} %bitcast.3, s32[8]{0:T(128)} %len_ref.1, bf16[8,16384]{1,0:T(8,128)(2,1)} %q_hbm.1, bf16[8,128,256]{2,1,0:T(8,128)(2,1)} %k_hbm.1, ...), custom_call_target="tpu_custom_call" | custom-call | tf_op jit(solution)/shard_map/pallas_call | solution.py:398
  45.4 1.6 %copy.15 = bf16[8,7168]{1,0:T(8,128)(2,1)} copy(bf16[8,7168]{1,0:T(8,128)(2,1)} %get-tuple-element.4) | data formatting | bytes 229376
  46.9 1.7 %copy.16 = bf16[8,16384]{1,0:T(8,128)(2,1)} copy(bf16[8,16384]{1,0:T(8,128)(2,1)} %get-tuple-element.5) | data formatting | bytes 524288

commit v3 on v2

--- a/solution.py
+++ b/solution.py
@@ -13,9 +13,10 @@
 ROWS = 8
 PIECES = 4
 CHUNKS = 7
+SUM_CHUNKS = 7
 AHEAD = 3
-GATHER_Y = 2
-GATHER_C = 4
+GATHER_Y = 3
+GATHER_C = 5
 SUM_C = 1
 SUM_Y = 4
 SUM_Z = 7
@@ -78,6 +79,7 @@
     i = attn % 2
     half = hid_ref.shape[1] // 2
     kc = half // CHUNKS
+    nc = half // SUM_CHUNKS
     blocks = 4 * outer
 
     def device(o2, i2, c2):
@@ -107,10 +109,10 @@
     def out_weights(k):
         copies = []
         for h in range(2):
-            cols = pl.ds(pl.multiple_of(h * half + k * kc, kc), kc)
+            cols = pl.ds(pl.multiple_of(h * half + k * nc, nc), nc)
             copies.append(
                 pltpu.make_async_copy(
-                    wd_hbm.at[:, cols], wd.at[k, :, pl.ds(h * kc, kc)], wd_sem.at[k, h]
+                    wd_hbm.at[:, cols], wd.at[k, :, pl.ds(h * nc, nc)], wd_sem.at[k, h]
                 )
             )
         return copies
@@ -220,7 +222,7 @@
             copy.start()
         return 0
 
-    lax.fori_loop(0, CHUNKS, start_out, 0)
+    lax.fori_loop(0, SUM_CHUNKS, start_out, 0)
 
     gate_acc[...] = jnp.zeros_like(gate_acc)
     up_acc[...] = jnp.zeros_like(up_acc)
@@ -312,26 +314,26 @@
     per_expert = outer // EXPERTS
 
     def sum_step(t, _):
-        @pl.when(t < CHUNKS)
+        @pl.when(t < SUM_CHUNKS)
         def _():
             for copy in out_weights(t):
                 copy.wait()
             down = jnp.dot(hidden[...], wd[t], preferred_element_type=F32)
-            low = down[:, :kc].reshape(blocks, ROWS, kc)
-            high = down[:, kc:].reshape(blocks, ROWS, kc)
+            low = down[:, :nc].reshape(blocks, ROWS, nc)
+            high = down[:, nc:].reshape(blocks, ROWS, nc)
             both = jnp.concatenate([low, high], axis=1).astype(BF16)
-            part[t] = both.reshape(2, 2 * outer, 2 * ROWS, kc)
+            part[t] = both.reshape(2, 2 * outer, 2 * ROWS, nc)
             rc_copy(t).start()
 
-        @pl.when((t >= SUM_C) & (t < CHUNKS + SUM_C))
+        @pl.when((t >= SUM_C) & (t < SUM_CHUNKS + SUM_C))
         def _():
             k = t - SUM_C
             rc_copy(k).wait_recv()
             total = part[k, c].astype(F32) + core_in[k].astype(F32)
-            sum_core[k] = total.astype(BF16).reshape(2, outer, 2 * ROWS, kc)
+            sum_core[k] = total.astype(BF16).reshape(2, outer, 2 * ROWS, nc)
             ry_copy(k).start()
 
-        @pl.when((t >= SUM_Y) & (t < CHUNKS + SUM_Y))
+        @pl.when((t >= SUM_Y) & (t < SUM_CHUNKS + SUM_Y))
         def _():
             k = t - SUM_Y
             ry_copy(k).wait_recv()
@@ -346,31 +348,37 @@
             k = t - SUM_Z
             for d in range(1, outer):
                 rz_copy(k, z_peer(d), z_peer(d), z_peer(d), d).wait_recv()
-            total = jnp.zeros((2 * ROWS, kc), F32)
+            total = jnp.zeros((2 * ROWS, nc), F32)
             for e in range(EXPERTS):
                 expert = z_in[k, e * per_expert].astype(F32)
                 for m in range(1, per_expert):
                     expert = expert + z_in[k, e * per_expert + m].astype(F32)
                 total = total + row_weight[e] * expert
-            ffn_ref[:, pl.ds(pl.multiple_of(k * kc, kc), kc)] = total[:ROWS].astype(BF16)
-            ffn_ref[:, pl.ds(pl.multiple_of(half + k * kc, kc), kc)] = total[ROWS:].astype(BF16)
-
-        return 0
-
-    lax.fori_loop(0, CHUNKS + SUM_Z, sum_step, 0)
+            ffn_ref[:, pl.ds(pl.multiple_of(k * nc, nc), nc)] = total[:ROWS].astype(BF16)
+            ffn_ref[:, pl.ds(pl.multiple_of(half + k * nc, nc), nc)] = total[ROWS:].astype(BF16)
+
+        return 0
+
+    lax.fori_loop(0, SUM_CHUNKS + SUM_Z, sum_step, 0)
 
     def drain(k, _):
         for d in range(1, outer):
             z_copy(k, o, d).wait_send()
-            rz_copy(k, z_peer(d), z_peer(d), o, d).wait_send()
         for d in range(outer):
             y_copy(k, i, z_peer(d)).wait_send()
         c_copy(k, c).wait_send()
+        return 0
+
+    lax.fori_loop(0, CHUNKS, drain, 0)
+
+    def drain_sums(k, _):
+        for d in range(1, outer):
+            rz_copy(k, z_peer(d), z_peer(d), o, d).wait_send()
         rc_copy(k).wait_send()
         ry_copy(k).wait_send()
         return 0
 
-    lax.fori_loop(0, CHUNKS, drain, 0)
+    lax.fori_loop(0, SUM_CHUNKS, drain_sums, 0)
 
 
 def on_device(
@@ -390,6 +398,7 @@
     units = w_gate.shape[1]
     outer = lax.axis_size("attn") // 2
     kc = features // 2 // CHUNKS
+    nc = features // 2 // SUM_CHUNKS
     blocks = 4 * outer
     vmem = pl.BlockSpec(memory_space=pltpu.VMEM)
     smem = pl.BlockSpec(memory_space=pltpu.SMEM)
@@ -406,7 +415,7 @@
         scratch_shapes=[
             pltpu.VMEM((CHUNKS, 2 * kc, units), BF16),
             pltpu.VMEM((CHUNKS, 2 * kc, units), BF16),
-            pltpu.VMEM((CHUNKS, units, 2 * kc), BF16),
+            pltpu.VMEM((SUM_CHUNKS, units, 2 * nc), BF16),
             pltpu.VMEM(queries.shape, BF16),
             pltpu.VMEM(key_cache.shape, BF16),
             pltpu.VMEM(value_cache.shape, BF16),
@@ -414,27 +423,27 @@
             pltpu.VMEM((blocks * ROWS, units), F32),
             pltpu.VMEM((blocks * ROWS, units), F32),
             pltpu.VMEM((blocks * ROWS, units), BF16),
-            pltpu.VMEM((CHUNKS, 2, 2 * outer, 2 * ROWS, kc), BF16),
-            pltpu.VMEM((CHUNKS, 2 * outer, 2 * ROWS, kc), BF16),
-            pltpu.VMEM((CHUNKS, 2, outer, 2 * ROWS, kc), BF16),
-            pltpu.VMEM((CHUNKS, outer, 2 * ROWS, kc), BF16),
-            pltpu.VMEM((CHUNKS, outer, 2 * ROWS, kc), BF16),
-            pltpu.VMEM((CHUNKS, outer, 2 * ROWS, kc), BF16),
+            pltpu.VMEM((SUM_CHUNKS, 2, 2 * outer, 2 * ROWS, nc), BF16),
+            pltpu.VMEM((SUM_CHUNKS, 2 * outer, 2 * ROWS, nc), BF16),
+            pltpu.VMEM((SUM_CHUNKS, 2, outer, 2 * ROWS, nc), BF16),
+            pltpu.VMEM((SUM_CHUNKS, outer, 2 * ROWS, nc), BF16),
+            pltpu.VMEM((SUM_CHUNKS, outer, 2 * ROWS, nc), BF16),
+            pltpu.VMEM((SUM_CHUNKS, outer, 2 * ROWS, nc), BF16),
             dma((3,)),
             dma((CHUNKS, 2, 2)),
-            dma((CHUNKS, 2)),
+            dma((SUM_CHUNKS, 2)),
             dma((CHUNKS, outer)),
             dma((CHUNKS, outer)),
             dma((CHUNKS, outer)),
             dma((CHUNKS, outer)),
             dma((CHUNKS,)),
             dma((CHUNKS,)),
-            dma((CHUNKS,)),
-            dma((CHUNKS,)),
-            dma((CHUNKS,)),
-            dma((CHUNKS,)),
-            dma((CHUNKS, outer)),
-            dma((CHUNKS, outer)),
+            dma((SUM_CHUNKS,)),
+            dma((SUM_CHUNKS,)),
+            dma((SUM_CHUNKS,)),
+            dma((SUM_CHUNKS,)),
+            dma((SUM_CHUNKS, outer)),
+            dma((SUM_CHUNKS, outer)),
         ],
         compiler_params=pltpu.CompilerParams(
             collective_id=0, has_side_effects=True, vmem_limit_bytes=60 * 2**20

time: 48.8 us -> 48.2 us (0.988)
  Pallas kernels: 44.7 us -> 44.1 us
    pallas_call x1, Pallas kernels: 44.7 us -> 44.1 us  [on_device(): pl.pallas_call(functools.partial(kernel, outer), out_shape=(jax.ShapeDtyp...]
where the time goes in v3:
time: 48.2 us; the launch traced here: 48 us
  Pallas kernels  44.1 us (91%)
  local copies, waits for them, and re-layouts  3.22 us (7%)
  between operations  0.64 us (1%)
    pallas_call x1, Pallas kernels, on_device(): pl.pallas_call(functools.partial(kernel, outer), out_shape=(jax.ShapeDtyp...  44.1 us
    unnamed x2, local copies, waits for them, and re-layouts  3.22 us

profile of v3, /device:TPU:0, one launch (start us, length us, event | category | flops | bytes accessed | tf_op | source)
XLA Modules:
  0.0 48.0 jit_solution(14657461478383895170)
XLA Ops:
  0.6 44.1 %shard_map.122 = (bf16[8,7168]{1,0:T(8,128)(2,1)}, bf16[8,16384]{1,0:T(8,128)(2,1)}) custom-call(bf16[8,7168]{1,0:T(8,128)(2,1)} %hid_ref.1, bf16[7168]{0:T(1024)(128)(2,1)} %gain_ref.1, s32[3,8]{1,0:T(4,128)} %bitcast.2, f32[3,8]{1,0:T(4,128)} %bitcast.3, s32[8]{0:T(128)} %len_ref.1, bf16[8,16384]{1,0:T(8,128)(2,1)} %q_hbm.1, bf16[8,128,256]{2,1,0:T(8,128)(2,1)} %k_hbm.1, ...), custom_call_target="tpu_custom_call" | custom-call | tf_op jit(solution)/shard_map/pallas_call | solution.py:407
  44.8 1.6 %copy.15 = bf16[8,7168]{1,0:T(8,128)(2,1)} copy(bf16[8,7168]{1,0:T(8,128)(2,1)} %get-tuple-element.4) | data formatting | bytes 229376
  46.3 1.7 %copy.16 = bf16[8,16384]{1,0:T(8,128)(2,1)} copy(bf16[8,16384]{1,0:T(8,128)(2,1)} %get-tuple-element.5) | data formatting | bytes 524288
